TPU v7x, 512 devices: a whole 4x8x8 slice. The times are simulated.
512 devices in a mesh: seq: 64 (over x, y, core), mp: 8 (over z).
Axes of the slice: x: 4, y: 8, z: 8, core: 2. Of those that a mesh axis runs over, the one named last changes fastest.
Arguments:
- token_ids: int32 [96, 2], replicated, may hold values from 0 to 25599
- prompt_lengths: int32 [6], replicated, may hold values from 1024 to 8192, as said below
- tail_lengths: int32 [96], replicated, may hold values from 32 to 256, as said below
- prompt_of: int32 [96], replicated, may hold values from 0 to 5, as said below
- page_table: int32 [96, 2], replicated, may hold values from 0 to 191, as said below
- prompt_keys: bfloat16 [49152, 6144], P('seq', 'mp'), may hold values from -240 to 240
- prompt_values: bfloat16 [49152, 6144], P('seq', 'mp'), may hold values from -12 to 12
- tail_keys: bfloat16 [24576, 6144], P('seq', 'mp'), may hold values from -240 to 240
- tail_values: bfloat16 [24576, 6144], P('seq', 'mp'), may hold values from -12 to 12
- norm_gain: bfloat16 [2, 7168], P(None, 'seq'), may hold values from 0.5 to 1.5
- norm_bias: bfloat16 [2, 7168], P(None, 'seq'), may hold values from -2 to 2
- qkv_weight: bfloat16 [7168, 3, 6144], P('seq', None, 'mp'), may hold values from -0.0625 to 0.0625
- qkv_bias: bfloat16 [3, 6144], P(None, 'mp'), may hold values from -2 to 2
- out_weight: bfloat16 [6144, 7168], P('mp', 'seq'), may hold values from -0.078125 to 0.078125
- out_bias: bfloat16 [7168], P('seq'), may hold values from -0.796875 to 0.796875
- embedding: bfloat16 [25600, 7168], P('mp', 'seq'), may hold values from -0.3984375 to 0.3984375
- score_weight: bfloat16 [7168], P('seq'), may hold values from -0.0625 to 0.0625
Outputs:
- hidden_states: bfloat16 [192, 7168], P(None, 'seq')
- score_values: float32 [96], replicated
- hidden_norms: float32 [192], replicated
- top_logits: float32 [96], replicated
Inputs may be any that keep to these rules, and one draw needn't show every extreme that they name: `prompt_lengths`: the longest prompt has exactly 8192 positions. `tail_lengths`: some continuation has exactly 256 tail tokens. `prompt_of`: each prompt is extended by 16 continuations or one more. `page_table`: all entries are distinct, so every pool page belongs to one continuation.
All inputs are finite; a program needn't handle non-finite values.
Results may differ from a plain program's by a relative error of at most 0.017.
The roundings to bfloat16 on the way count: a program that leaves them out, or rounds other values in their place, can miss the bound.
Values may be sent and summed in bfloat16 or wider, within the bound.
A program may use at most 128 MiB of HBM per device.

v0:
```python
import math

import jax
import jax.numpy as jnp
from jax import lax
from jax.sharding import PartitionSpec as P

D = 7168
HD = 128
PAGE = 128


epsilon = 1e-05
neg_fill = -1e30


def combine_parts(first, second):
    first_max, first_total, first_sum = first
    second_max, second_total, second_sum = second
    greatest = jnp.maximum(first_max, second_max)
    first_factor = jnp.exp(first_max - greatest)
    second_factor = jnp.exp(second_max - greatest)
    totals = first_total * first_factor + second_total * second_factor
    summed = first_sum * first_factor[..., None] + second_sum * second_factor[..., None]
    return (greatest, totals, summed)


def attend(queries, keys, values, valid, score_scale):
    scores = (
        jnp.einsum("cthe,nhe->chtn", queries, keys, preferred_element_type=jnp.float32)
        * score_scale
    )
    masked = valid[:, None, :, :]
    scores = jnp.where(masked, scores, neg_fill)
    greatest = jnp.max(scores, axis=-1)
    weights = jnp.where(masked, jnp.exp(scores - greatest[..., None]), 0.0)
    totals = jnp.sum(weights, axis=-1)
    summed = jnp.einsum(
        "chtn,nhe->chte", weights.astype(jnp.bfloat16), values, preferred_element_type=jnp.float32
    )
    return (greatest, totals, summed)


def per_device(
    token_ids,
    prompt_lengths,
    tail_lengths,
    prompt_of,
    page_table,
    prompt_keys,
    prompt_values,
    tail_keys,
    tail_values,
    norm_gain,
    norm_bias,
    qkv_weight,
    qkv_bias,
    out_weight,
    out_bias,
    embedding,
    score_weight,
):
    cont_count = token_ids.shape[0]
    row_count = 2 * cont_count
    vocab_local = embedding.shape[0]
    seq_index = lax.axis_index("seq")
    mp_index = lax.axis_index("mp")
    local_ids = token_ids.reshape(row_count) - mp_index * vocab_local
    inside = (local_ids >= 0) & (local_ids < vocab_local)
    picked = jnp.take(embedding, jnp.clip(local_ids, 0, vocab_local - 1), axis=0).astype(
        jnp.float32
    )
    picked = jnp.where(inside[:, None], picked, 0.0)
    inputs = lax.psum(picked, "mp").astype(jnp.bfloat16).astype(jnp.float32)
    input_sum, input_sq = lax.psum(
        (jnp.sum(inputs, axis=1), jnp.sum(inputs * inputs, axis=1)), "seq"
    )
    average = input_sum / D
    variance = input_sq / D - average * average
    gains = norm_gain.astype(jnp.float32)
    offsets = norm_bias.astype(jnp.float32)
    normed = (
        (inputs - average[:, None]) * lax.rsqrt(variance + epsilon)[:, None] * gains[0] + offsets[0]
    ).astype(jnp.bfloat16)
    partial_qkv = jnp.einsum("rd,dke->rke", normed, qkv_weight, preferred_element_type=jnp.float32)
    bias_rows = qkv_bias.astype(jnp.float32)
    qkv = (lax.psum(partial_qkv, "seq") + bias_rows).astype(jnp.bfloat16)
    head_local = qkv.shape[2] // HD
    queries = qkv[:, 0].reshape(cont_count, 2, head_local, HD)
    new_keys = qkv[:, 1].reshape(cont_count, 2, head_local, HD)
    new_values = qkv[:, 2].reshape(cont_count, 2, head_local, HD)
    score_scale = 1.0 / math.sqrt(HD)
    prompt_count = prompt_keys.shape[0]
    starts = jnp.cumsum(prompt_lengths) - prompt_lengths
    prompt_pick = (
        prompt_of[:, None] == jnp.arange(prompt_lengths.shape[0], dtype=jnp.int32)[None, :]
    ).astype(jnp.int32)
    begin = jnp.sum(prompt_pick * starts[None, :], axis=1)
    finish = begin + jnp.sum(prompt_pick * prompt_lengths[None, :], axis=1)
    position = seq_index * prompt_count + jnp.arange(prompt_count, dtype=jnp.int32)
    prompt_mask = (position[None, :] >= begin[:, None]) & (position[None, :] < finish[:, None])
    prompt_part = attend(
        queries,
        prompt_keys.reshape(prompt_count, head_local, HD),
        prompt_values.reshape(prompt_count, head_local, HD),
        prompt_mask[:, None, :],
        score_scale,
    )
    tail_count = tail_keys.shape[0]
    pages_local = tail_count // PAGE
    page_ids = seq_index * pages_local + jnp.arange(pages_local, dtype=jnp.int32)
    owned = page_table[:, :, None] == page_ids[None, None, :]
    offsets_tail = (
        jnp.arange(2, dtype=jnp.int32)[:, None] * PAGE + jnp.arange(PAGE, dtype=jnp.int32)[None, :]
    )
    filled = offsets_tail[None, :, :] < tail_lengths[:, None, None]
    tail_mask = jnp.any(owned[:, :, :, None] & filled[:, :, None, :], axis=1).reshape(
        cont_count, tail_count
    )
    tail_part = attend(
        queries,
        tail_keys.reshape(tail_count, head_local, HD),
        tail_values.reshape(tail_count, head_local, HD),
        tail_mask[:, None, :],
        score_scale,
    )
    local_part = combine_parts(prompt_part, tail_part)
    greatest = lax.pmax(local_part[0], "seq")
    factor = jnp.exp(local_part[0] - greatest)
    totals, summed = lax.psum((local_part[1] * factor, local_part[2] * factor[..., None]), "seq")
    merged = (greatest, totals, summed)
    self_scores = (
        jnp.einsum("cthe,cshe->chts", queries, new_keys, preferred_element_type=jnp.float32)
        * score_scale
    )
    causal = (jnp.arange(2, dtype=jnp.int32)[:, None] >= jnp.arange(2, dtype=jnp.int32)[None, :])[
        None, None, :, :
    ]
    self_scores = jnp.where(causal, self_scores, neg_fill)
    self_max = jnp.max(self_scores, axis=-1)
    self_weights = jnp.where(causal, jnp.exp(self_scores - self_max[..., None]), 0.0)
    self_total = jnp.sum(self_weights, axis=-1)
    self_sum = jnp.einsum(
        "chts,cshe->chte",
        self_weights.astype(jnp.bfloat16),
        new_values,
        preferred_element_type=jnp.float32,
    )
    greatest, totals, summed = combine_parts(merged, (self_max, self_total, self_sum))
    attended = (
        (summed / totals[..., None])
        .transpose(0, 2, 1, 3)
        .reshape(row_count, head_local * HD)
        .astype(jnp.bfloat16)
    )
    projected = jnp.dot(attended, out_weight, preferred_element_type=jnp.float32)
    hidden = inputs + lax.psum(projected, "mp") + out_bias.astype(jnp.float32)
    hidden_sum, hidden_sq = lax.psum(
        (jnp.sum(hidden, axis=1), jnp.sum(hidden * hidden, axis=1)), "seq"
    )
    hidden_norms = jnp.sqrt(hidden_sq / D)
    last_rows = hidden.reshape(cont_count, 2, hidden.shape[1])[:, 1]
    last_average = hidden_sum.reshape(cont_count, 2)[:, 1] / D
    last_variance = hidden_sq.reshape(cont_count, 2)[:, 1] / D - last_average * last_average
    final = (
        (last_rows - last_average[:, None]) * lax.rsqrt(last_variance + epsilon)[:, None] * gains[1]
        + offsets[1]
    ).astype(jnp.bfloat16)
    score_values = lax.psum(jnp.dot(final, score_weight, preferred_element_type=jnp.float32), "seq")
    logit_share = lax.psum_scatter(
        lax.dot_general(
            embedding, final, (((1,), (1,)), ((), ())), preferred_element_type=jnp.float32
        ),
        "seq",
        scatter_dimension=0,
        tiled=True,
    )
    top_logits = lax.pmax(jnp.max(logit_share, axis=0), ("seq", "mp"))
    return (hidden.astype(jnp.bfloat16), score_values, hidden_norms, top_logits)


def solution(mesh):
    return jax.shard_map(
        per_device,
        mesh=mesh,
        in_specs=(
            P(),
            P(),
            P(),
            P(),
            P(),
            P("seq", "mp"),
            P("seq", "mp"),
            P("seq", "mp"),
            P("seq", "mp"),
            P(None, "seq"),
            P(None, "seq"),
            P("seq", None, "mp"),
            P(None, "mp"),
            P("mp", "seq"),
            P("seq"),
            P("mp", "seq"),
            P("seq"),
        ),
        out_specs=(P(None, "seq"), P(), P(), P()),
        check_vma=False,
    )
```

profile of v0, /device:TPU:1, one launch (start us, length us, event | category | flops | bytes accessed | tf_op | source)
XLA Modules:
  0.0 1449.8 jit_solution(1172715131099909362)
XLA Ops:
  7.3 0.7 subtract_clamp_fusion
  8.4 0.7 compare_and_fusion.2
  9.1 1.5 copy.159
  10.9 0.8 gather_fusion
  11.8 30.5 %psum.70 = bf16[192,112]{1,0:T(8,128)(2,1)S(1)} all-reduce(f32[192,112]{1,0:T(8,128)S(1)} %convert_select_fusion), channel_id=1, replica_groups=mesh['seq'=64,'mp'=8] {'mp'}, use_global_device_ids=true, to_apply=%region_0.1 | all-reduce | flops 21504 | bytes 129024 | tf_op jit(solution)/shard_map/psum | solution.py:74
  42.5 0.5 slice_bitcast_fusion
  43.1 131.9 %all-reduce.2 = (f32[192]{0:T(256)S(1)}, f32[192]{0:T(256)S(1)}) all-reduce(f32[192]{0:T(256)S(1)} %get-tuple-element.9, f32[192]{0:T(256)S(1)} %get-tuple-element.8), channel_id=1, replica_groups=mesh['seq'=64,'mp'=8] {'seq'}, use_global_device_ids=true, to_apply=%region_7.8 | all-reduce | flops 384 | bytes 3072 | tf_op jit(solution)/shard_map/psum | solution.py:75
  175.0 1.7 fusion.51
  176.9 1.1 copy.166
  178.2 0.6 copy.160
  178.8 2.4 copy.163
  181.2 1.1 copy.169
  182.8 0.6 copy_bitcast_fusion
  183.5 178.7 %all-reduce.8.cloned.1.call-done = f32[192,3,768]{2,0,1:T(8,128)} async-done(((f32[192,3,768]{2,0,1:T(8,128)}), f32[192,3,768]{2,0,1:T(8,128)}) %all-reduce.8.cloned.1.call-update) | async-done | bytes 1769488 | tf_op jit(solution)/shard_map/psum | solution.py:87
  362.2 1.6 add_convert_fusion
  363.8 0.8 fusion.77
  364.6 0.3 reshape_squeeze.10
  364.9 0.3 reshape_squeeze.9
  365.3 0.7 fusion.37
  366.0 0.3 copy.173
  366.4 0.7 fusion.74
  367.1 1.8 bitcast_reduce_fusion.1
  368.9 1.3 fusion.16
  370.2 0.9 bitcast_reduce_fusion
  371.1 0.6 max.21
  371.7 1.1 copy-done.1
  372.9 1.8 fusion.2
  374.7 128.4 %pmax.14 = f32[96,6,2]{0,2,1:T(2,128)} all-reduce(f32[96,6,2]{0,2,1:T(2,128)} %max.21), channel_id=1, replica_groups=mesh['seq'=64,'mp'=8] {'seq'}, use_global_device_ids=true, to_apply=%region_12.13 | all-reduce | flops 1152 | bytes 9216 | tf_op jit(solution)/shard_map/pmax | solution.py:128
  503.0 1.4 add_multiply_fusion
  504.4 130.1 %psum.75 = f32[96,6,2]{0,2,1:T(2,128)} all-reduce(f32[96,6,2]{0,2,1:T(2,128)} %get-tuple-element.22), channel_id=1, replica_groups=mesh['seq'=64,'mp'=8] {'seq'}, use_global_device_ids=true, to_apply=%region_17.18 | all-reduce | flops 1152 | bytes 9216 | tf_op jit(solution)/shard_map/psum | solution.py:130
  634.5 3.3 fusion.18
  638.0 1.7 fusion.15
  640.2 0.3 reshape_squeeze.11
  640.6 0.7 fusion.35
  641.4 184.1 %all-reduce.10.cloned.1.call-done = f32[96,6,2,128]{3,0,2,1:T(8,128)} async-done(((f32[96,6,2,128]{3,0,2,1:T(8,128)}), f32[96,6,2,128]{3,0,2,1:T(8,128)}) %all-reduce.10.cloned.1.call-update) | async-done | bytes 589840 | tf_op jit(solution)/shard_map/psum | solution.py:130
  825.5 1.7 fusion.34
  827.4 0.9 fusion.31
  828.4 74.0 %all-reduce.12.cloned.1.call-done = f32[192,112]{1,0:T(8,128)} async-done(((f32[192,112]{1,0:T(8,128)}), f32[192,112]{1,0:T(8,128)}) %all-reduce.12.cloned.1.call-update) | async-done | bytes 86032 | tf_op jit(solution)/shard_map/psum | solution.py:157
  902.4 1.0 fusion.72
  903.6 245.9 %all-reduce.1 = (f32[96,2]{1,0:T(8,128)S(1)}, f32[192]{0:T(256)S(1)}) all-reduce(f32[96,2]{1,0:T(8,128)S(1)} %reshape.242, f32[192]{0:T(256)S(1)} %get-tuple-element.5), channel_id=1, replica_groups=mesh['seq'=64,'mp'=8] {'seq'}, use_global_device_ids=true, to_apply=%region_21.22 | all-reduce | flops 384 | bytes 3072 | tf_op jit(solution)/shard_map/psum | solution.py:158
  1150.0 1.4 convolution_bitcast_fusion
  1151.4 1.3 dynamic-slice
  1153.3 0.6 convert_element_type.67
  1154.1 129.6 %psum.79 = f32[96]{0:T(128)} all-reduce(f32[96]{0:T(128)S(1)} %convolution_bitcast_fusion.2), channel_id=1, replica_groups=mesh['seq'=64,'mp'=8] {'seq'}, use_global_device_ids=true, to_apply=%region_24.25 | all-reduce | flops 96 | bytes 768 | tf_op jit(solution)/shard_map/psum | solution.py:169
  1283.7 0.6 multiply_sqrt_fusion
  1284.3 58.6 %all-reduce.14.cloned.1.call-done = f32[3200,96]{0,1:T(8,128)} async-done(((f32[3200,96]{0,1:T(8,128)}), f32[3200,96]{0,1:T(8,128)}) %all-reduce.14.cloned.1.call-update) | async-done | bytes 1228816
  1342.8 1.1 dynamic-slice_reduce_fusion
  1343.9 99.3 %pmax.15 = f32[96]{0:T(128)} all-reduce(f32[96]{0:T(128)S(1)} %dynamic-slice_reduce_fusion), channel_id=1, replica_groups=mesh['seq'=64,'mp'=8] {'seq','mp'}, use_global_device_ids=true, to_apply=%region_27.28 | all-reduce | flops 96 | bytes 768 | tf_op jit(solution)/shard_map/pmax | solution.py:178
  (116 shorter events, 3.7 us)
Async XLA Ops:
  7.2 167.8 %copy-start = (bf16[112,3,768]{2,0,1:T(8,128)(2,1)S(1)}, bf16[112,3,768]{2,0,1:T(8,128)(2,1)}, u32[]{:S(2)}) copy-start(bf16[112,3,768]{2,0,1:T(8,128)(2,1)} %param.28) | copy-start | bytes 1548292
  7.2 35.1 %copy-start.32 = (bf16[2,112]{1,0:T(2,128)(2,1)S(1)}, bf16[2,112]{1,0:T(2,128)(2,1)}, u32[]{:S(2)}) copy-start(bf16[2,112]{1,0:T(2,128)(2,1)} %param.27) | copy-start | bytes 1348
  7.2 35.2 %copy-start.33 = (bf16[2,112]{1,0:T(2,128)(2,1)S(1)}, bf16[2,112]{1,0:T(2,128)(2,1)}, u32[]{:S(2)}) copy-start(bf16[2,112]{1,0:T(2,128)(2,1)} %param.26) | copy-start | bytes 1348
  7.2 355.0 %all-reduce.8.cloned.1.call-start = ((), (), s32[]{:S(2)}) async-start(), calls=%async_computation | async-start | bytes 3538944 | tf_op jit(solution)/shard_map/psum | solution.py:87
  42.3 134.4 %copy-start.8 = (bf16[192,112]{1,0:T(8,128)(2,1)}, bf16[192,112]{1,0:T(8,128)(2,1)S(1)}, u32[]{:S(2)}) copy-start(bf16[192,112]{1,0:T(8,128)(2,1)S(1)} %psum.70) | copy-start | bytes 129028
  175.0 1.8 copy-start.22
  175.0 1.9 copy-start.10
  176.7 1.3 copy-start.28
  176.7 1.5 copy-start.5
  176.7 648.8 %all-reduce.10.cloned.1.call-start = ((), (), s32[]{:S(2)}) async-start(), calls=%async_computation.1 | async-start | bytes 1179648 | tf_op jit(solution)/shard_map/psum | solution.py:130
  178.2 3.1 copy-start.11
  178.8 3.5 copy-start.27
  178.8 3.6 copy-start.29
  178.8 3.7 copy-start.30
  365.3 1.9 copy-start.3
  366.3 2.6 copy-start.13
  366.4 0.7 copy-start.16
  367.1 3.1 copy-start.4
  371.1 1.8 copy-start.1
  372.9 261.7 %copy-start.6 = (bf16[768,768]{0,1:T(8,128)(2,1)S(1)}, bf16[768,768]{0,1:T(8,128)(2,1)}, u32[]{:S(2)}) copy-start(bf16[768,768]{0,1:T(8,128)(2,1)} %copy.163) | copy-start | bytes 3538948
  634.5 3.3 copy-start.12
  634.5 3.3 copy-start.14
  634.5 3.3 copy-start.23
  634.5 3.4 copy-start.24
  637.9 2.0 copy-start.19
  637.9 2.0 copy-start.17
  637.9 2.0 copy-start.18
  637.9 2.0 copy-start.20
  637.9 2.0 copy-start.21
  637.9 2.3 copy-start.7
  639.6 262.7 %all-reduce.12.cloned.1.call-start = ((), (), s32[]{:S(2)}) async-start(), calls=%async_computation.2 | async-start | bytes 196608 | tf_op jit(solution)/shard_map/psum | solution.py:157
  640.6 186.8 %copy-start.15 = (bf16[768,112]{0,1:T(8,128)(2,1)S(1)}, bf16[768,112]{0,1:T(8,128)(2,1)}, u32[]{:S(2)}) copy-start(bf16[768,112]{0,1:T(8,128)(2,1)} %param.30) | copy-start | bytes 516100
  641.3 187.0 %copy-start.34 = (bf16[112]{0:T(256)(128)(2,1)S(1)}, bf16[112]{0:T(256)(128)(2,1)}, u32[]{:S(2)}) copy-start(bf16[112]{0:T(256)(128)(2,1)} %param.31) | copy-start | bytes 676
  641.3 261.0 %copy-start.9 = (bf16[192,112]{1,0:T(8,128)(2,1)S(1)}, bf16[192,112]{1,0:T(8,128)(2,1)}, u32[]{:S(2)}) copy-start(bf16[192,112]{1,0:T(8,128)(2,1)} %copy-done.8) | copy-start | bytes 129028
  641.4 508.5 %copy-start.25 = (f32[112]{0:T(128)S(1)}, f32[112]{0:T(128)}, u32[]{:S(2)}) copy-start(f32[112]{0:T(128)} %get-tuple-element.31) | copy-start | bytes 1348
  641.4 508.5 %copy-start.26 = (f32[112]{0:T(128)S(1)}, f32[112]{0:T(128)}, u32[]{:S(2)}) copy-start(f32[112]{0:T(128)} %get-tuple-element.40) | copy-start | bytes 1348
  825.5 324.5 %copy-start.2 = (bf16[3200,112]{0,1:T(8,128)(2,1)S(1)}, bf16[3200,112]{0,1:T(8,128)(2,1)}, u32[]{:S(2)}) copy-start(bf16[3200,112]{0,1:T(8,128)(2,1)} %param.32) | copy-start | bytes 2150404
  828.3 514.5 %all-reduce.14.cloned.1.call-start = ((), (), s32[]{:S(2)}) async-start(), calls=%async_computation.3 | async-start | bytes 2457600
  1149.7 4.3 copy-start.31
Sparse Core Ops, SparseCore 0:
  176.8 185.3 all-reduce.7
  639.8 185.7 all-reduce.9
  828.4 73.9 all-reduce.11
  1151.5 191.2 all-reduce.13
where the time goes:
time: 1450 us
  blocking collectives  896 us (62%)
  waiting for transfers between devices  495 us (34%)
  other arithmetic  15.3 us (1%)
  between operations  15 us (1%)
  local copies, waits for them, and re-layouts  14.7 us (1%)
    psum x1, blocking collectives, per_device(): lax.psum((jnp.sum(hidden, axis=1), jnp.sum(hidden * hidden, axis=1)), 'seq')  246 us
    psum x1, waiting for transfers between devices, per_device(): lax.psum((local_part[1] * factor, local_part[2] * factor[..., None]), 'seq')  184 us
    psum x1, waiting for transfers between devices, per_device(): qkv = (lax.psum(partial_qkv, 'seq') + bias_rows).astype(jnp.bfloat16)  179 us
    psum x1, blocking collectives, per_device(): lax.psum((jnp.sum(inputs, axis=1), jnp.sum(inputs * inputs, axis=1)), 'seq')  132 us
    psum x1, blocking collectives, per_device(): lax.psum((local_part[1] * factor, local_part[2] * factor[..., None]), 'seq')  130 us
    psum x1, blocking collectives, per_device(): lax.psum(jnp.dot(final, score_weight, preferred_element_type=jnp.float32)...  130 us
    pmax x1, blocking collectives, per_device(): greatest = lax.pmax(local_part[0], 'seq')  128 us
    pmax x1, blocking collectives, per_device(): top_logits = lax.pmax(jnp.max(logit_share, axis=0), ('seq', 'mp'))  99.3 us
  transfers between devices with their start and end apart: 4, of which 4 were waited for; matrix products, arithmetic and copies ran while one was open for 1% of the time, Pallas kernels for 0%

commit v1 on v0

v1 whole, which is shorter than its diff:
```python
import math

import jax
import jax.numpy as jnp
from jax import lax
from jax.experimental import pallas as pl
from jax.experimental.pallas import tpu as pltpu
from jax.sharding import PartitionSpec as P

D = 7168
HD = 128
PAGE = 128
NX, NY, NC, NZ = 4, 8, 2, 8
CONT = 96
R = 256
DL = 112
HALF = 384
VL = 3200
HC = 48
WX = 896
EPS = 1e-05
NEG = -1e30
LEAST = -1e29
LOW = -3e38
SCALE = 1.0 / math.sqrt(HD)
BF = jnp.bfloat16
F32 = jnp.float32
HI = lax.Precision.HIGHEST
MESH = pl.DeviceIdType.MESH

NN = (((1,), (0,)), ((), ()))
NT = (((1,), (1,)), ((), ()))


def mm(a, b, dims=NN, precision=None):
    return lax.dot_general(a, b, dims, precision=precision, preferred_element_type=F32)


def iota(shape, axis):
    return lax.broadcasted_iota(jnp.int32, shape, axis)


def round_bf(v):
    return v.astype(BF).astype(F32)


def kernel(
    lens,
    tok,
    tails,
    prompt,
    pages,
    gain,
    offset,
    qkv_bias,
    out_bias,
    score_weight,
    pk_hbm,
    pv_hbm,
    tk_hbm,
    tv_hbm,
    w_hbm,
    wo_hbm,
    emb_hbm,
    hid_out,
    score_out,
    norm_out,
    top_out,
    pk,
    pv,
    tk,
    tv,
    w,
    wo,
    emb,
    bias,
    normed,
    gp,
    za_s,
    za_r,
    zi,
    st_z,
    st_c,
    st_y,
    qc_s,
    qc_r,
    q_f,
    qx_s,
    qx_r,
    qy_s,
    qy_r,
    qay,
    qac,
    kc_s,
    kc_r,
    kv_f,
    kx_s,
    kx_r,
    ky_s,
    ky_r,
    o_f,
    ml_f,
    oc_s,
    oc_r,
    ox_s,
    ox_r,
    oy_s,
    oy_r,
    aay,
    aac,
    hz_s,
    hz_r,
    hs_c,
    hs_y,
    hid,
    fin,
    nrm,
    lc_s,
    lc_r,
    l_f,
    lx_s,
    lx_r,
    ly_s,
    ly_r,
    sc_c,
    sc_y,
    mx_c,
    mx_y,
    mx_z,
    ssem,
    rsem,
    lsem,
):
    seq = lax.axis_index("seq")
    mz = lax.axis_index("mp")
    x = seq // 16
    y = (seq // 2) % 8
    c = seq % 2
    k = x * 2 + c
    oc = 1 - c

    def dev_c(d):
        return (x * 16 + y * 2 + (c + d) % 2, mz)

    def dev_x(d):
        return (((x + d) % NX) * 16 + y * 2 + c, mz)

    def dev_y(d):
        return (x * 16 + ((y + d) % NY) * 2 + c, mz)

    def dev_k(d):
        t = (k + d) % 8
        return ((t // 2) * 16 + y * 2 + t % 2, mz)

    def dev_z(d):
        return (seq, (mz + d) % NZ)

    waits = []

    def gather(s, buf, at, dev, n):
        for d in range(1, n):
            pltpu.make_async_remote_copy(
                src_ref=buf.at[at],
                dst_ref=buf.at[at],
                send_sem=ssem.at[s],
                recv_sem=rsem.at[s],
                device_id=dev(d),
                device_id_type=MESH,
            ).start()
        waits.append((s, buf.at[pl.ds(0, n - 1)]))

    def gathered(s, buf, n):
        part = buf.at[pl.ds(0, n - 1)]
        pltpu.make_async_copy(part, part, rsem.at[s]).wait()

    def scatter(s, src, dst, dev, at, n):
        for d in range(1, n):
            pltpu.make_async_remote_copy(
                src_ref=src.at[at(d)],
                dst_ref=dst.at[d - 1],
                send_sem=ssem.at[s],
                recv_sem=rsem.at[s],
                device_id=dev(d),
                device_id_type=MESH,
            ).start()
        waits.append((s, dst))

    def scattered(s, dst):
        pltpu.make_async_copy(dst, dst, rsem.at[s]).wait()

    def to_x(d):
        return (x + d) % NX

    def to_y(d):
        return (y + d) % NY

    def to_z(d):
        return (mz + d) % NZ

    def zero(d):
        return 0

    loads = [
        pltpu.make_async_copy(a, b, lsem.at[i])
        for i, (a, b) in enumerate(
            (
                (emb_hbm, emb),
                (w_hbm, w),
                (pk_hbm, pk),
                (tk_hbm, tk),
                (pv_hbm, pv),
                (tv_hbm, tv),
                (wo_hbm, wo),
            )
        )
    ]
    for load in loads:
        load.start()

    barrier = pltpu.get_barrier_semaphore()
    for dev in (dev_k, dev_y, dev_z):
        for d in range(1, 8):
            pl.semaphore_signal(barrier, inc=1, device_id=dev(d), device_id_type=MESH)

    row = iota((R, CONT), 0)
    slot = row % 8
    of_cont = ((row // 8) * 3 + slot // 2 == iota((R, CONT), 1)) & (slot < 6)
    i8 = iota((8, CONT), 0)
    facts = jnp.where(i8 == 0, prompt[...], 0)
    facts = jnp.where(i8 == 1, tails[...], facts)
    facts = jnp.where(i8 == 2, pages[0:1, :], facts)
    facts = jnp.where(i8 == 3, pages[1:2, :], facts)
    facts = jnp.where(i8 == 4, tok[0:1, :], facts)
    facts = jnp.where(i8 == 5, tok[1:2, :], facts)
    facts = mm(jnp.where(of_cont, 1.0, 0.0).astype(F32), facts.astype(F32), NT, HI)
    facts = (facts + 0.5).astype(jnp.int32)
    slot1 = iota((R, 1), 0) % 8
    real = slot1 < 6
    ids = jnp.where(slot1 % 2 == 0, facts[:, 4:5], facts[:, 5:6])
    ids = jnp.where(real, ids - mz * VL, -1)

    loads[0].wait()
    pick_chunk = 640

    def pick(i, total):
        at = pl.multiple_of(i * pick_chunk, pick_chunk)
        lane = iota((R, pick_chunk), 1) + at
        hot = jnp.where(lane == ids, 1.0, 0.0).astype(BF)
        return total + mm(hot, emb[:, pl.ds(at, pick_chunk)], NT)

    picked = lax.fori_loop(0, VL // pick_chunk, pick, jnp.zeros((R, DL), F32))
    wide = jnp.concatenate([picked, jnp.zeros((R, 128 - DL), F32)], axis=1)
    za_s[...] = wide.reshape(NZ, 32, 128).astype(BF)
    ones = jnp.ones((8, 128), F32)
    i128 = iota((8, 128), 0)
    squares = wide * wide
    stat = jnp.where(i128 == 0, mm(ones, wide[:128], NT, HI), 0.0)
    stat = jnp.where(i128 == 1, mm(ones, wide[128:], NT, HI), stat)
    stat = jnp.where(i128 == 2, mm(ones, squares[:128], NT, HI), stat)
    stat = jnp.where(i128 == 3, mm(ones, squares[128:], NT, HI), stat)
    st_z[mz] = stat

    pl.semaphore_wait(barrier, 21)
    gather(1, st_z, mz, dev_z, NZ)
    scatter(0, za_s, za_r, dev_z, to_z, NZ)

    gp[...] = jnp.zeros_like(gp)
    gp[0:2, :DL] = gain[...].astype(F32)
    gp[2:4, :DL] = offset[...].astype(F32)
    gp[4:5, :DL] = out_bias[...].astype(F32)
    gp[5:6, :DL] = score_weight[...].astype(F32)

    whose = facts[:, 0:1]
    begin = jnp.zeros((R, 1), jnp.int32)
    length = jnp.zeros((R, 1), jnp.int32)
    for j in range(6):
        begin = begin + jnp.where(whose > j, lens[j], 0)
        length = jnp.where(whose == j, lens[j], length)
    begin = begin - seq * 768
    finish = jnp.where(real, begin + length, begin)
    place = iota((R, 768), 1)
    bias[:, :768] = jnp.where((place >= begin) & (place < finish), 0.0, NEG).astype(F32)
    kept = jnp.where(real, facts[:, 1:2], 0)
    lane = iota((R, PAGE), 1)
    for j in range(3):
        page = seq * 3 + j
        held = jnp.where(facts[:, 2:3] == page, kept, 0)
        held = jnp.where(facts[:, 3:4] == page, kept - PAGE, held)
        bias[:, 768 + j * PAGE : 768 + (j + 1) * PAGE] = jnp.where(lane < held, 0.0, NEG).astype(F32)

    gathered(1, st_z, NZ)
    total = st_z[0]
    for i in range(1, 8):
        total = total + st_z[i]
    st_c[k] = total
    gather(2, st_c, k, dev_k, 8)

    scattered(0, za_r)
    own = za_s[mz].astype(F32)
    for i in range(7):
        own = own + za_r[i].astype(F32)
    zi[mz] = own.astype(BF)
    gather(4, zi, mz, dev_z, NZ)

    gathered(2, st_c, 8)
    total = st_c[0]
    for i in range(1, 8):
        total = total + st_c[i]
    st_y[y] = total
    gather(3, st_y, y, dev_y, NY)
    gathered(4, zi, NZ)
    loads[1].wait()
    gathered(3, st_y, NY)
    total = st_y[0]
    for i in range(1, 8):
        total = total + st_y[i]
    mean = total[0:2] * (1.0 / D)
    rstd = lax.rsqrt(total[2:4] * (1.0 / D) - mean * mean + EPS)
    eye = jnp.where(iota((128, 128), 0) == iota((128, 128), 1), 1.0, 0.0).astype(F32)
    for b in range(2):
        both = jnp.where(i128 == 0, mean[b : b + 1], jnp.where(i128 == 1, rstd[b : b + 1], 0.0))
        cols = mm(eye, both, NT, HI)
        part = zi[4 * b : 4 * b + 4].reshape(128, 128).astype(F32)
        part = (part - cols[:, 0:1]) * cols[:, 1:2] * gp[0:1, :] + gp[2:3, :]
        normed[b * 128 : (b + 1) * 128, :] = part.astype(BF)

    mine_at = pl.multiple_of(c * HALF, 128)
    other_at = pl.multiple_of(oc * HALF, 128)
    rows = normed[:, :DL]
    qc_s[0] = mm(rows, w[0, :, pl.ds(other_at, HALF)]).astype(BF)
    scatter(5, qc_s, qc_r, dev_c, zero, 2)
    q_f[...] = mm(rows, w[0, :, pl.ds(mine_at, HALF)])
    for j in range(2):
        kc_s[0, j] = mm(rows, w[1 + j, :, pl.ds(other_at, HALF)]).astype(BF)
    scattered(5, qc_r)
    full = q_f[...] + qc_r[0].astype(F32)
    q_f[...] = full
    qx_s[...] = full.reshape(NX, 64, HALF).astype(BF)
    scatter(6, qx_s, qx_r, dev_x, to_x, NX)
    scatter(10, kc_s, kc_r, dev_c, zero, 2)
    for j in range(2):
        kv_f[j] = mm(rows, w[1 + j, :, pl.ds(mine_at, HALF)])
    my_rows = pl.ds(pl.multiple_of(x * 64, 64), 64)
    scattered(6, qx_r)
    part = q_f[my_rows, :]
    for i in range(3):
        part = part + qx_r[i].astype(F32)
    qy_s[...] = part.reshape(NY, 8, HALF)
    scatter(7, qy_s, qy_r, dev_y, to_y, NY)
    scattered(10, kc_r)
    for j in range(2):
        full = kv_f[j] + kc_r[0, j].astype(F32)
        kv_f[j] = full
        for i in range(NX):
            kx_s[i, j] = full[i * 64 : (i + 1) * 64].astype(BF)
    scattered(7, qy_r)
    query = qy_s[y]
    for i in range(7):
        query = query + qy_r[i]
    query = round_bf(query + qkv_bias[0:1, pl.ds(mine_at, HALF)].astype(F32))
    qay[y] = query
    gather(8, qay, y, dev_y, NY)
    gathered(8, qay, NY)
    qac[k] = qay[...].reshape(64, HALF).astype(BF)
    gather(9, qac, k, dev_k, 8)
    for load in loads[2:6]:
        load.wait()
    gathered(9, qac, 8)
    scatter(11, kx_s, kx_r, dev_x, to_x, NX)

    lane_r = iota((R, 128), 1)

    def attend(half, which):
        ml_f[which] = jnp.zeros((R, 128), F32)

        def head(hh, carry):
            hl = pl.ds(pl.multiple_of(hh * HD, HD), HD)
            hg = pl.ds(pl.multiple_of(half * HALF + hh * HD, HD), HD)
            q = jnp.concatenate([qac[2 * i + half, :, hl] for i in range(NX)], axis=0)
            s1 = mm(q, pk[:, hg], NT) * SCALE + bias[:, :768]
            s2 = mm(q, tk[:, hg], NT) * SCALE + bias[:, 768:]
            m = jnp.maximum(jnp.max(s1, axis=1, keepdims=True), jnp.max(s2, axis=1, keepdims=True))
            m = jnp.maximum(m, LEAST)
            m1 = round_bf(m)
            m2 = round_bf(m - m1)
            base = m1 + m2
            e1 = jnp.exp(s1 - base)
            e2 = jnp.exp(s2 - base)
            l = jnp.sum(e1, axis=1, keepdims=True) + jnp.sum(e2, axis=1, keepdims=True)
            o_f[which, :, hl] = mm(e1.astype(BF), pv[:, hg]) + mm(e2.astype(BF), tv[:, hg])
            ml = ml_f[which]
            ml = jnp.where(lane_r == hh, base, ml)
            ml_f[which] = jnp.where(lane_r == 3 + hh, l, ml)
            return carry

        lax.fori_loop(0, 3, head, 0)

    def pack(ml, lanes):
        first = round_bf(ml)
        second = ml - first
        n = ml.shape[0]
        out = jnp.where(lanes < 6, first, 0.0)
        return jnp.where((lanes >= 64) & (lanes < 70), pltpu.roll(second, 64, 1), out)

    def unpack(t):
        return t + pltpu.roll(t, 64, 1)

    attend(oc, 0)
    oc_s[0, :, :HALF] = o_f[0].astype(BF)
    oc_s[0, :, HALF:] = pack(ml_f[0], lane_r).astype(BF)
    scatter(13, oc_s, oc_r, dev_c, zero, 2)

    scattered(11, kx_r)
    for j in range(2):
        part = kv_f[j, my_rows, :]
        for i in range(3):
            part = part + kx_r[i, j].astype(F32)
        for i in range(NY):
            ky_s[i, j] = part[i * 8 : (i + 1) * 8]
    scatter(12, ky_s, ky_r, dev_y, to_y, NY)
    attend(c, 1)

    def merge(parts, lanes, extra=None):
        greatest = parts[0][1]
        for _, ml in parts[1:]:
            greatest = jnp.maximum(greatest, ml)
        if extra is not None:
            greatest = jnp.maximum(greatest, extra)
        sums, totals = [None] * 3, None
        for o, ml in parts:
            f = jnp.exp(ml - greatest)
            t = pltpu.roll(f, 3, 1) * ml
            totals = t if totals is None else totals + t
            for h in range(3):
                term = o[:, h * HD : (h + 1) * HD] * f[:, h : h + 1]
                sums[h] = term if sums[h] is None else sums[h] + term
        return sums, jnp.where(lanes < 3, greatest, totals), greatest

    scattered(13, oc_r)
    sums, ml, _ = merge(
        [
            (o_f[1], jnp.where(lane_r < 6, ml_f[1], 0.0)),
            (
                oc_r[0, :, :HALF].astype(F32),
                jnp.where(lane_r < 6, unpack(oc_r[0, :, HALF:].astype(F32)), 0.0),
            ),
        ],
        lane_r,
    )
    packed = pack(ml, lane_r)
    for h in range(3):
        o_f[0, :, h * HD : (h + 1) * HD] = sums[h]
        ox_s[:, :, h * HD : (h + 1) * HD] = sums[h].reshape(NX, 64, HD).astype(BF)
    ml_f[0] = ml
    ox_s[:, :, HALF:] = packed.reshape(NX, 64, 128).astype(BF)
    scatter(14, ox_s, ox_r, dev_x, to_x, NX)
    lane_x = iota((64, 128), 1)
    scattered(14, ox_r)
    parts = [(o_f[0, my_rows, :], jnp.where(lane_x < 6, ml_f[0, my_rows, :], 0.0))]
    for i in range(3):
        parts.append(
            (
                ox_r[i, :, :HALF].astype(F32),
                jnp.where(lane_x < 6, unpack(ox_r[i, :, HALF:].astype(F32)), 0.0),
            )
        )
    sums, ml, _ = merge(parts, lane_x)
    for h in range(3):
        oy_s[:, :, h * HD : (h + 1) * HD] = sums[h].reshape(NY, 8, HD)
    oy_s[:, :, HALF:] = jnp.where(lane_x < 6, ml, 0.0).reshape(NY, 8, 128)
    scatter(15, oy_s, oy_r, dev_y, to_y, NY)

    scattered(12, ky_r)
    key = ky_s[y, 0]
    value = ky_s[y, 1]
    for i in range(7):
        key = key + ky_r[i, 0]
        value = value + ky_r[i, 1]
    key = round_bf(key + qkv_bias[1:2, pl.ds(mine_at, HALF)].astype(F32))
    value = round_bf(value + qkv_bias[2:3, pl.ds(mine_at, HALF)].astype(F32))
    lane_8 = iota((8, 128), 1)
    odd = i128 % 2 == 1
    key_before = pltpu.roll(key, 1, 0)
    value_before = pltpu.roll(value, 1, 0)
    same = jnp.full((8, 128), NEG, F32)
    before = jnp.full((8, 128), NEG, F32)
    for h in range(3):
        hs = slice(h * HD, (h + 1) * HD)
        a = jnp.sum(query[:, hs] * key[:, hs], axis=1, keepdims=True) * SCALE
        b = jnp.sum(query[:, hs] * key_before[:, hs], axis=1, keepdims=True) * SCALE
        same = jnp.where(lane_8 == h, a, same)
        before = jnp.where((lane_8 == h) & odd, b, before)

    scattered(15, oy_r)
    parts = [(oy_s[y, :, :HALF], oy_s[y, :, HALF:])]
    for i in range(7):
        parts.append((oy_r[i, :, :HALF], oy_r[i, :, HALF:]))
    sums, ml, greatest = merge(parts, lane_8, jnp.maximum(same, before))
    w_same = jnp.exp(same - greatest)
    w_before = jnp.exp(before - greatest)
    totals = pltpu.roll(ml, 125, 1) + w_same + w_before
    w_same = round_bf(w_same)
    w_before = round_bf(w_before)
    for h in range(3):
        hs = slice(h * HD, (h + 1) * HD)
        o = sums[h] + w_same[:, h : h + 1] * value[:, hs] + w_before[:, h : h + 1] * value_before[:, hs]
        aay[y, :, hs] = o / totals[:, h : h + 1]
    gather(16, aay, y, dev_y, NY)
    loads[6].wait()
    gathered(16, aay, NY)
    aac[k] = aay[...].reshape(64, HALF).astype(BF)
    gather(17, aac, k, dev_k, 8)
    gathered(17, aac, 8)
    out = jnp.zeros((R, DL), F32)
    for half in range(2):
        part = jnp.concatenate([aac[2 * i + half] for i in range(NX)], axis=0)
        out = out + mm(part, wo[:, half * HALF : (half + 1) * HALF], NT)
    out = jnp.concatenate([out, jnp.zeros((R, 128 - DL), F32)], axis=1)
    hz_s[...] = out.reshape(NZ, 32, 128).astype(BF)
    scatter(18, hz_s, hz_r, dev_z, to_z, NZ)
    scattered(18, hz_r)
    hidden = hz_s[mz].astype(F32)
    for i in range(7):
        hidden = hidden + hz_r[i].astype(F32)
    hidden = hidden + zi[mz].astype(F32) + gp[4:5, :]
    tall = jnp.concatenate([hidden, jnp.zeros((96, 128), F32)], axis=0)
    hs_c[k] = jnp.where(i128 == 0, mm(ones, tall, NT, HI), mm(ones, tall * tall, NT, HI))
    gather(19, hs_c, k, dev_k, 8)
    hid[mz] = hidden.astype(BF)
    gather(21, hid, mz, dev_z, NZ)
    gathered(19, hs_c, 8)
    total = hs_c[0]
    for i in range(1, 8):
        total = total + hs_c[i]
    hs_y[y] = total
    gather(20, hs_y, y, dev_y, NY)
    gathered(20, hs_y, NY)
    total = hs_y[0]
    for i in range(1, 8):
        total = total + hs_y[i]
    mean = total[0:1] * (1.0 / D)
    square = total[1:2] * (1.0 / D)
    rstd = lax.rsqrt(square - mean * mean + EPS)
    both = jnp.where(i128 == 0, mean, jnp.where(i128 == 1, rstd, 0.0))
    cols = mm(eye[:32], both, NT, HI)
    final = ((hidden - cols[:, 0:1]) * cols[:, 1:2] * gp[1:2, :] + gp[3:4, :]).astype(BF)
    i16 = iota((16, 32), 0)
    last = (iota((16, 32), 1) == 8 * (i16 // 3) + 2 * (i16 % 3) + 1) & (i16 < 12)
    fin[mz] = mm(jnp.where(last, 1.0, 0.0).astype(BF), final).astype(BF)
    gather(22, fin, mz, dev_z, NZ)
    nrm[mz] = jnp.where(i128 == 0, jnp.sqrt(square), 0.0)
    gather(23, nrm, mz, dev_z, NZ)
    gathered(22, fin, NZ)

    finals = fin[...].reshape(128, 128)

    def rows_of(n, start):
        cont = iota((n, 128), 0) + start
        hot = iota((n, 128), 1) == (cont // 12) * 16 + cont % 12
        return mm(jnp.where(hot & (cont < CONT), 1.0, 0.0).astype(BF), finals).astype(BF)

    lc_s[0] = mm(rows_of(HC, oc * HC)[:, :DL], emb[...]).astype(BF)
    scatter(24, lc_s, lc_r, dev_c, zero, 2)
    sc_c[k] = mm(jnp.broadcast_to(gp[5:6, :], (8, 128)).astype(BF), rows_of(128, 0), NT)
    gather(27, sc_c, k, dev_k, 8)
    l_f[...] = mm(rows_of(HC, c * HC)[:, :DL], emb[...])
    scattered(24, lc_r)
    full = l_f[...] + lc_r[0].astype(F32)
    l_f[...] = full
    for i, t in enumerate((0, 7, 14, 18)):
        lx_s[i] = full[:, t * 128 : t * 128 + WX].astype(BF)
    scatter(25, lx_s, lx_r, dev_x, to_x, NX)
    gathered(27, sc_c, 8)
    total = sc_c[0]
    for i in range(1, 8):
        total = total + sc_c[i]
    sc_y[y] = total
    gather(28, sc_y, y, dev_y, NY)

    gathered(21, hid, NZ)
    out_row = iota((192, R), 0)
    back = iota((192, R), 1) == (out_row // 6) * 8 + out_row % 6
    states = mm(jnp.where(back, 1.0, 0.0).astype(BF), hid[...].reshape(R, 128))
    hid_out[...] = states[:, :DL].astype(BF)
    gathered(23, nrm, NZ)
    norms = jnp.zeros((8, 192), F32)
    for i in range(NZ):
        col = iota((128, 192), 1)
        at = (col // 6) * 8 + col % 6 - i * 32
        norms = norms + mm(nrm[i], jnp.where(iota((128, 192), 0) == at, 1.0, 0.0).astype(F32), NN, HI)
    norm_out[...] = norms[0:1]

    scattered(25, lx_r)
    at = pl.multiple_of((7 * x - 3 * (x // 3)) * 128, 128)
    part = l_f[:, pl.ds(at, WX)]
    for i in range(3):
        part = part + lx_r[i].astype(F32)
    for i in range(7):
        ly_s[i] = part[:, i * 128 : (i + 1) * 128].astype(BF)

    def word_tile(d):
        t = (y + d) % NY
        return t - t // 7

    scatter(26, ly_s, ly_r, dev_y, word_tile, NY)
    gathered(28, sc_y, NY)
    total = sc_y[0]
    for i in range(1, 8):
        total = total + sc_y[i]
    score_out[...] = total[0:1, :CONT]
    scattered(26, ly_r)
    logits = ly_s[word_tile(0)].astype(F32)
    for i in range(7):
        logits = logits + ly_r[i].astype(F32)
    top = jnp.max(logits, axis=1, keepdims=True)
    lane_h = iota((HC, 128), 1) - c * HC
    row_h = iota((HC, 128), 0)
    top = jnp.sum(jnp.where(lane_h == row_h, top, 0.0), axis=0, keepdims=True)
    lane_1 = lane_8 - c * HC
    best = jnp.where((lane_1 >= 0) & (lane_1 < HC), top, LOW)
    for s, buf, at, dev in ((29, mx_c, k, dev_k), (30, mx_y, y, dev_y), (31, mx_z, mz, dev_z)):
        buf[at] = best
        gather(s, buf, at, dev, 8)
        gathered(s, buf, 8)
        best = buf[0]
        for i in range(1, 8):
            best = jnp.maximum(best, buf[i])
    top_out[...] = best[0:1, :CONT]

    for s, part in waits:
        pltpu.make_async_copy(part, part, ssem.at[s]).wait()


def per_device(
    token_ids,
    prompt_lengths,
    tail_lengths,
    prompt_of,
    page_table,
    prompt_keys,
    prompt_values,
    tail_keys,
    tail_values,
    norm_gain,
    norm_bias,
    qkv_weight,
    qkv_bias,
    out_weight,
    out_bias,
    embedding,
    score_weight,
):
    vm = pl.BlockSpec(memory_space=pltpu.VMEM)
    hbm = pl.BlockSpec(memory_space=pl.ANY)
    sm = pl.BlockSpec(memory_space=pltpu.SMEM)

    def b(*shape):
        return pltpu.VMEM(shape, BF)

    def f(*shape):
        return pltpu.VMEM(shape, F32)

    scratch = [
        b(768, 768),
        b(768, 768),
        b(384, 768),
        b(384, 768),
        b(3, DL, 768),
        b(DL, 768),
        b(DL, VL),
        f(R, 1152),
        b(R, 128),
        f(8, 128),
        b(8, 32, 128),
        b(7, 32, 128),
        b(8, 32, 128),
        f(8, 8, 128),
        f(8, 8, 128),
        f(8, 8, 128),
        b(1, R, HALF),
        b(1, R, HALF),
        f(R, HALF),
        b(NX, 64, HALF),
        b(3, 64, HALF),
        f(NY, 8, HALF),
        f(7, 8, HALF),
        f(NY, 8, HALF),
        b(8, 64, HALF),
        b(1, 2, R, HALF),
        b(1, 2, R, HALF),
        f(2, R, HALF),
        b(NX, 2, 64, HALF),
        b(3, 2, 64, HALF),
        f(NY, 2, 8, HALF),
        f(7, 2, 8, HALF),
        f(2, R, HALF),
        f(2, R, 128),
        b(1, R, 512),
        b(1, R, 512),
        b(NX, 64, 512),
        b(3, 64, 512),
        f(NY, 8, 512),
        f(7, 8, 512),
        f(NY, 8, HALF),
        b(8, 64, HALF),
        b(8, 32, 128),
        b(7, 32, 128),
        f(8, 8, 128),
        f(8, 8, 128),
        b(8, 32, 128),
        b(8, 16, 128),
        f(8, 8, 128),
        b(1, HC, VL),
        b(1, HC, VL),
        f(HC, VL),
        b(NX, HC, WX),
        b(3, HC, WX),
        b(7, HC, 128),
        b(7, HC, 128),
        f(8, 8, 128),
        f(8, 8, 128),
        f(8, 8, 128),
        f(8, 8, 128),
        f(8, 8, 128),
        pltpu.SemaphoreType.DMA((32,)),
        pltpu.SemaphoreType.DMA((32,)),
        pltpu.SemaphoreType.DMA((7,)),
    ]
    hidden, score, norms, top = pl.pallas_call(
        kernel,
        out_shape=(
            jax.ShapeDtypeStruct((192, DL), BF),
            jax.ShapeDtypeStruct((1, CONT), F32),
            jax.ShapeDtypeStruct((1, 192), F32),
            jax.ShapeDtypeStruct((1, CONT), F32),
        ),
        in_specs=[sm] + [vm] * 9 + [hbm] * 7,
        out_specs=(vm, vm, vm, vm),
        scratch_shapes=scratch,
        compiler_params=pltpu.CompilerParams(
            collective_id=0, has_side_effects=True, vmem_limit_bytes=40 * 2**20
        ),
    )(
        prompt_lengths,
        token_ids.T,
        tail_lengths.reshape(1, CONT),
        prompt_of.reshape(1, CONT),
        page_table.T,
        norm_gain,
        norm_bias,
        qkv_bias,
        out_bias.reshape(1, DL),
        score_weight.reshape(1, DL),
        prompt_keys,
        prompt_values,
        tail_keys,
        tail_values,
        qkv_weight.transpose(1, 0, 2),
        out_weight.T,
        embedding.T,
    )
    return hidden, score.reshape(CONT), norms.reshape(192), top.reshape(CONT)


def solution(mesh):
    return jax.shard_map(
        per_device,
        mesh=mesh,
        in_specs=(
            P(),
            P(),
            P(),
            P(),
            P(),
            P("seq", "mp"),
            P("seq", "mp"),
            P("seq", "mp"),
            P("seq", "mp"),
            P(None, "seq"),
            P(None, "seq"),
            P("seq", None, "mp"),
            P(None, "mp"),
            P("mp", "seq"),
            P("seq"),
            P("mp", "seq"),
            P("seq"),
        ),
        out_specs=(P(None, "seq"), P(), P(), P()),
        check_vma=False,
    )
```

time: 1450 us -> 147 us (0.10)
  blocking collectives: 896 us -> 0 us
  waiting for transfers between devices: 495 us -> 0 us
  Pallas kernels: 0 us -> 129 us
  other arithmetic: 15.3 us -> 0 us
    psum x5 -> x0, blocking collectives: 668 us -> none  [the longest x1 246 us: per_device(): lax.psum((jnp.sum(hidden, axis=1), jnp.sum(hidden * hidden, axis=1)), 'seq')]
    psum x3 -> x0, waiting for transfers between devices: 437 us -> none  [the longest x1 184 us: per_device(): lax.psum((local_part[1] * factor, local_part[2] * factor[..., None]), 'seq')]
    pmax x2 -> x0, blocking collectives: 228 us -> none  [the longest x1 128 us: per_device(): greatest = lax.pmax(local_part[0], 'seq')]
    pallas_call x0 -> x1, Pallas kernels: none -> 129 us  [per_device(): pl.pallas_call(kernel, out_shape=(jax.ShapeDtypeStruct((192, DL), BF), ja...]
    unnamed x5 -> x0, waiting for transfers between devices: 58.6 us -> none
  transfers between devices with their start and end apart: 4 -> 0, of which waited for: 4 -> 0; matrix products, arithmetic and copies ran while one was open for 1% -> 0% of each run, Pallas kernels for 0% -> 0%
where the time goes in v1:
time: 147 us
  Pallas kernels  129 us (88%)
  local copies, waits for them, and re-layouts  16.6 us (11%)
    pallas_call x1, Pallas kernels, per_device(): pl.pallas_call(kernel, out_shape=(jax.ShapeDtypeStruct((192, DL), BF), ja...  129 us
    unnamed x38, local copies, waits for them, and re-layouts  16.6 us

profile of v1, /device:TPU:1, one launch (start us, length us, event | category | flops | bytes accessed | tf_op | source)
XLA Modules:
  0.0 146.7 jit_solution(11915426342869112179)
XLA Ops:
  0.6 0.0 copy-start
  0.6 1.3 copy-done
  1.9 0.0 copy-start.1
  1.9 1.3 copy-done.1
  3.2 0.0 copy-start.2
  3.2 1.1 copy-done.2
  4.3 0.0 copy-start.3
  4.3 1.1 copy-done.3
  5.4 0.0 copy-start.4
  5.4 1.1 copy-done.4
  6.4 0.0 copy-start.5
  6.4 1.0 copy-done.5
  7.5 0.0 copy-start.6
  7.5 0.9 copy-done.6
  8.4 0.0 copy-start.7
  8.4 0.7 copy-done.7
  9.1 0.0 copy-start.8
  9.1 0.7 copy-done.8
  9.7 0.0 copy-start.9
  9.8 0.7 copy-done.9
  10.4 0.0 copy-start.10
  10.4 0.7 copy-done.10
  11.1 0.0 copy-start.11
  11.1 0.7 copy-done.11
  11.7 0.0 copy-start.12
  11.7 0.7 copy-done.12
  12.4 0.0 copy-start.13
  12.4 0.7 copy-done.13
  13.1 0.0 copy-start.14
  13.1 0.7 copy-done.14
  13.7 0.0 copy-start.15
  13.7 0.7 copy-done.15
  14.4 0.0 copy-start.16
  14.4 0.7 copy-done.16
  15.0 129.4 %shard_map.192 = (bf16[192,112]{1,0:T(8,128)(2,1)S(1)}, f32[1,96]{1,0:T(1,128)S(1)}, f32[1,192]{1,0:T(1,128)S(1)}, f32[1,96]{1,0:T(1,128)S(1)}) custom-call(s32[6]{0:T(128)S(1)} %copy-done.10, s32[2,96]{1,0:T(2,128)S(1)} %bitcast.15, s32[1,96]{1,0:T(1,128)S(1)} %bitcast.18, s32[1,96]{1,0:T(1,128)S(1)} %bitcast.19, s32[2,96]{1,0:T(2,128)S(1)} %bitcast.16, ...), custom_call_target="tpu_custom_call" | custom-call | tf_op jit(solution)/shard_map/pallas_call | solution.py:729
  144.5 0.6 copy.25
  145.1 0.5 copy.26
  145.6 0.6 copy.27
  146.2 0.5 copy.28
Async XLA Ops:
  0.6 1.3 copy-start
  1.9 1.3 copy-start.1
  3.2 1.1 copy-start.2
  4.3 1.1 copy-start.3
  5.4 1.1 copy-start.4
  6.4 1.0 copy-start.5
  7.5 0.9 copy-start.6
  8.4 0.7 copy-start.7
  9.1 0.7 copy-start.8
  9.7 0.7 copy-start.9
  10.4 0.7 copy-start.10
  11.1 0.7 copy-start.11
  11.7 0.7 copy-start.12
  12.4 0.7 copy-start.13
  13.1 0.7 copy-start.14
  13.7 0.7 copy-start.15
  14.4 0.7 copy-start.16

commit v2 on v1

v2 whole, which is shorter than its diff:
```python
import math

import jax
import jax.numpy as jnp
from jax import lax
from jax.experimental import pallas as pl
from jax.experimental.pallas import tpu as pltpu
from jax.sharding import PartitionSpec as P

D = 7168
HD = 128
PAGE = 128
NX, NY, NC, NZ = 4, 8, 2, 8
CONT = 96
R = 256
DL = 112
HALF = 384
VL = 3200
HC = 48
TILES = 25
PLANE = NX * NY
NP = NC * NZ
EPS = 1e-05
NEG = -1e30
LEAST = -1e29
LOW = -3e38
SCALE = 1.0 / math.sqrt(HD)
BF = jnp.bfloat16
F32 = jnp.float32
MESH = pl.DeviceIdType.MESH

NN = (((1,), (0,)), ((), ()))
NT = (((1,), (1,)), ((), ()))


def mm(a, b, dims=NN):
    return lax.dot_general(a, b, dims, preferred_element_type=F32)


def iota(shape, axis):
    return lax.broadcasted_iota(jnp.int32, shape, axis)


def to_row(col):
    n = col.shape[0]
    return jnp.sum(jnp.where(iota((n, 128), 0) == iota((n, 128), 1), col, 0.0), axis=0, keepdims=True)


def to_col(row, n):
    return jnp.sum(jnp.where(iota((n, 128), 0) == iota((n, 128), 1), row, 0.0), axis=1, keepdims=True)


def round_bf(v):
    return v.astype(BF).astype(F32)


def kernel(
    lens_hbm,
    tok_hbm,
    tails_hbm,
    prompt_hbm,
    pages_hbm,
    gain_hbm,
    offset_hbm,
    qkv_bias_hbm,
    out_bias_hbm,
    score_weight_hbm,
    pk_hbm,
    pv_hbm,
    tk_hbm,
    tv_hbm,
    w_hbm,
    wo_hbm,
    emb_hbm,
    hid_out,
    score_out,
    norm_out,
    top_out,
    lens,
    tok,
    tails,
    prompt,
    pages,
    gain,
    offset,
    qkv_bias,
    out_bias,
    score_weight,
    pk,
    pv,
    tk,
    tv,
    w,
    wo,
    emb,
    bias,
    normed,
    gp,
    za_s,
    za_r,
    zi,
    gp_o,
    w_o,
    emb_o,
    st_p,
    st_z,
    q_f,
    qp_s,
    qp_r,
    qap,
    qac,
    kv_f,
    kp_s,
    kp_r,
    o_f,
    ml_f,
    oc_s,
    oc_r,
    op_s,
    op_r,
    aap,
    aac,
    hz_s,
    hz_r,
    hs_c,
    hs_p,
    hid,
    fin,
    nrm,
    l_f,
    lp_s,
    lp_r,
    mx_p,
    mx_z,
    ssem,
    rsem,
    lsem,
):
    seq = lax.axis_index("seq")
    mz = lax.axis_index("mp")
    x = seq // 16
    y = (seq // 2) % 8
    c = seq % 2
    p = x * NY + y
    oc = 1 - c
    pair = mz * NC + c
    pair_o = mz * NC + oc

    def dev_c(d):
        return (x * 16 + y * 2 + (c + d) % 2, mz)

    def far(v, n, t):
        return lax.rem(v + n // 2 + ((t + 1) // 2) * (1 - 2 * (t % 2)), n)

    def chips(visit):
        def along(i, carry):
            tx = lax.rem(x + 2 + lax.div(i + 1, 2) * (1 - 2 * lax.rem(i, 2)), NX)
            for t in range(NY - 1):
                visit(i * 8 + t, tx, far(y, NY, t))
            return carry

        lax.fori_loop(0, NX, along, 0)
        for i in range(NX - 1):
            visit(i * 8 + NY - 1, far(x, NX, i), y)

    def dev_chip(tx, ty):
        return (tx * 16 + ty * 2 + c, mz)

    def dev_pair(d):
        t = (pair + d) % NP
        return (x * 16 + y * 2 + t % NC, t // NC)

    def dev_z(d):
        return (seq, (mz + d) % NZ)

    waits = []

    def gather(s, buf, at, dev, n):
        for d in range(1, n):
            pltpu.make_async_remote_copy(
                src_ref=buf.at[at],
                dst_ref=buf.at[at],
                send_sem=ssem.at[s],
                recv_sem=rsem.at[s],
                device_id=dev(d),
                device_id_type=MESH,
            ).start()
        waits.append((s, buf.at[pl.ds(0, n - 1)]))

    def gathered(s, buf, n):
        part = buf.at[pl.ds(0, n - 1)]
        pltpu.make_async_copy(part, part, rsem.at[s]).wait()

    def scatter(s, src, dst, dev, at, n):
        for d in range(1, n):
            pltpu.make_async_remote_copy(
                src_ref=src.at[at(d)],
                dst_ref=dst.at[d - 1],
                send_sem=ssem.at[s],
                recv_sem=rsem.at[s],
                device_id=dev(d),
                device_id_type=MESH,
            ).start()
        waits.append((s, dst))

    def scattered(s, dst):
        pltpu.make_async_copy(dst, dst, rsem.at[s]).wait()

    def gather_p(s, buf):
        def send(j, tx, ty):
            pltpu.make_async_remote_copy(
                src_ref=buf.at[p],
                dst_ref=buf.at[p],
                send_sem=ssem.at[s],
                recv_sem=rsem.at[s],
                device_id=dev_chip(tx, ty),
                device_id_type=MESH,
            ).start()

        chips(send)
        waits.append((s, buf.at[pl.ds(0, PLANE - 1)]))

    def scatter_p(s, src, dst, at):
        def send(j, tx, ty):
            pltpu.make_async_remote_copy(
                src_ref=src.at[at(tx * NY + ty)],
                dst_ref=dst.at[j],
                send_sem=ssem.at[s],
                recv_sem=rsem.at[s],
                device_id=dev_chip(tx, ty),
                device_id_type=MESH,
            ).start()

        chips(send)
        waits.append((s, dst))

    def same_chip(t):
        return t

    def to_z(d):
        return (mz + d) % NZ

    def zero(d):
        return 0

    barrier = pltpu.get_barrier_semaphore()

    def greet(j, tx, ty):
        pl.semaphore_signal(barrier, inc=1, device_id=dev_chip(tx, ty), device_id_type=MESH)

    chips(greet)
    for d in range(1, NP):
        pl.semaphore_signal(barrier, inc=1, device_id=dev_pair(d), device_id_type=MESH)

    loads = [
        pltpu.make_async_copy(a, b, lsem.at[i])
        for i, (a, b) in enumerate(
            (
                (lens_hbm, lens),
                (tok_hbm, tok),
                (tails_hbm, tails),
                (prompt_hbm, prompt),
                (pages_hbm, pages),
                (gain_hbm, gain),
                (offset_hbm, offset),
                (qkv_bias_hbm, qkv_bias),
                (out_bias_hbm, out_bias),
                (score_weight_hbm, score_weight),
                (emb_hbm, emb),
                (w_hbm, w),
                (pk_hbm, pk),
                (tk_hbm, tk),
                (pv_hbm, pv),
                (tv_hbm, tv),
                (wo_hbm, wo),
            )
        )
    ]
    for load in loads:
        load.start()

    for load in loads[:10]:
        load.wait()
    row = iota((R, CONT), 0)
    slot = row % 8
    of_cont = ((row // 8) * 3 + slot // 2 == iota((R, CONT), 1)) & (slot < 6)
    slot1 = iota((R, 1), 0) % 8
    real = slot1 < 6

    def of_row(v):
        v = jnp.sum(jnp.where(of_cont, v.astype(F32), 0.0), axis=1, keepdims=True)
        return (v + 0.5).astype(jnp.int32)

    ids = of_row(jnp.where(slot % 2 == 0, tok[0:1, :], tok[1:2, :]))
    ids = jnp.where(real, ids - mz * VL, -1)

    loads[10].wait()
    pick_chunk = 640

    def pick(i, total):
        at = pl.multiple_of(i * pick_chunk, pick_chunk)
        lane = iota((R, pick_chunk), 1) + at
        hot = jnp.where(lane == ids, 1.0, 0.0).astype(BF)
        return total + mm(hot, emb[:, pl.ds(at, pick_chunk)], NT)

    picked = lax.fori_loop(0, VL // pick_chunk, pick, jnp.zeros((R, DL), F32))
    wide = jnp.concatenate([picked, jnp.zeros((R, 128 - DL), F32)], axis=1)
    za_s[...] = wide.reshape(NZ, 32, 128).astype(BF)
    squares = jnp.sum(wide * wide, axis=1, keepdims=True)
    plain = jnp.sum(wide, axis=1, keepdims=True)
    for b in range(2):
        st_p[p, b : b + 1] = to_row(plain[b * 128 : (b + 1) * 128])
        st_p[p, 2 + b : 3 + b] = to_row(squares[b * 128 : (b + 1) * 128])

    pl.semaphore_wait(barrier, PLANE - 1 + NP - 1)
    scatter(0, za_s, za_r, dev_z, to_z, NZ)
    gather_p(2, st_p)

    gp[...] = jnp.zeros_like(gp)
    gp[0:2, :DL] = gain[...].astype(F32)
    gp[2:4, :DL] = offset[...].astype(F32)
    gp[4:5, :DL] = out_bias[...].astype(F32)
    gp[5:6, :DL] = score_weight[...].astype(F32)

    mine_at = pl.multiple_of(c * HALF, 128)
    other_at = pl.multiple_of(oc * HALF, 128)
    loads[11].wait()

    def lend(s, src, dst):
        pltpu.make_async_remote_copy(
            src_ref=src,
            dst_ref=dst,
            send_sem=ssem.at[s],
            recv_sem=rsem.at[s],
            device_id=dev_c(1),
            device_id_type=MESH,
        ).start()
        waits.append((s, dst))

    lend(7, gp, gp_o)
    lend(5, w.at[:, :, pl.ds(other_at, HALF)], w_o)

    whose = of_row(prompt[...])
    begin = jnp.zeros((R, 1), jnp.int32)
    length = jnp.zeros((R, 1), jnp.int32)
    for j in range(6):
        begin = begin + jnp.where(whose > j, lens[0:1, j : j + 1], 0)
        length = jnp.where(whose == j, lens[0:1, j : j + 1], length)
    begin = begin - seq * 768
    finish = jnp.where(real, begin + length, begin)
    place = iota((R, 768), 1)
    bias[:, :768] = jnp.where((place >= begin) & (place < finish), 0.0, NEG).astype(F32)
    kept = jnp.where(real, of_row(tails[...]), 0)
    page0 = of_row(pages[0:1, :])
    page1 = of_row(pages[1:2, :])
    lane = iota((R, PAGE), 1)
    for j in range(3):
        page = seq * 3 + j
        held = jnp.where(page0 == page, kept, 0)
        held = jnp.where(page1 == page, kept - PAGE, held)
        bias[:, 768 + j * PAGE : 768 + (j + 1) * PAGE] = jnp.where(lane < held, 0.0, NEG).astype(F32)

    scattered(0, za_r)
    own = za_s[mz].astype(F32)
    for i in range(7):
        own = own + za_r[i].astype(F32)
    zi[pair] = own.astype(BF)
    gather(4, zi, pair, dev_pair, NP)
    gathered(2, st_p, PLANE)
    st_z[pair] = jnp.sum(st_p[...], axis=0)
    gather(3, st_z, pair, dev_pair, NP)
    scattered(7, gp_o)
    scattered(5, w_o)
    gathered(4, zi, NP)
    gathered(3, st_z, NP)
    total = jnp.sum(st_z[...], axis=0)
    mean = total[0:2] * (1.0 / D)
    rstd = lax.rsqrt(total[2:4] * (1.0 / D) - mean * mean + EPS)
    for b in range(2):
        mean_col = to_col(mean[b : b + 1], 128)
        rstd_col = to_col(rstd[b : b + 1], 128)
        for o, core, g in ((0, c, gp), (1, oc, gp_o)):
            part = jnp.concatenate([zi[NC * (4 * b + i) + core] for i in range(4)], axis=0)
            part = (part.astype(F32) - mean_col) * rstd_col
            normed[o, b * 128 : (b + 1) * 128, :] = (part * g[0:1, :] + g[2:3, :]).astype(BF)

    rows = normed[0, :, :DL]
    rows_o = normed[1, :, :DL]
    full = mm(rows, w[0, :, pl.ds(mine_at, HALF)]) + mm(rows_o, w_o[0])
    q_f[...] = full
    qp_s[...] = full.reshape(PLANE, 8, HALF).astype(BF)
    scatter_p(6, qp_s, qp_r, same_chip)
    lend(24, emb, emb_o)
    for j in range(2):
        full = mm(rows, w[1 + j, :, pl.ds(mine_at, HALF)]) + mm(rows_o, w_o[1 + j])
        kv_f[j] = full
        kp_s[:, j] = full.reshape(PLANE, 8, HALF).astype(BF)
    my_rows = pl.ds(pl.multiple_of(p * 8, 8), 8)
    scattered(6, qp_r)
    query = q_f[my_rows, :] + jnp.sum(qp_r[...].astype(F32), axis=0)
    query = round_bf(query + qkv_bias[0:1, pl.ds(mine_at, HALF)].astype(F32))
    qap[p] = query.astype(BF)
    gather_p(8, qap)
    scatter_p(11, kp_s, kp_r, same_chip)
    for load in loads[12:16]:
        load.wait()
    ml_f[...] = jnp.zeros_like(ml_f)
    gathered(8, qap, PLANE)
    qac[c] = qap[...]
    gather(9, qac, c, dev_c, NC)

    lane_r = iota((R, 128), 1)

    def attend(half, which, low, high):
        def head(hh, carry):
            hl = pl.ds(pl.multiple_of(hh * HD, HD), HD)
            hg = pl.ds(pl.multiple_of(half * HALF + hh * HD, HD), HD)
            q = qac[half, :, :, hl].astype(F32).reshape(R, HD).astype(BF)
            s1 = mm(q, pk[:, hg], NT) * SCALE + bias[:, :768]
            s2 = mm(q, tk[:, hg], NT) * SCALE + bias[:, 768:]
            m = jnp.maximum(jnp.max(s1, axis=1, keepdims=True), jnp.max(s2, axis=1, keepdims=True))
            m = jnp.maximum(m, LEAST)
            m1 = round_bf(m)
            m2 = round_bf(m - m1)
            base = m1 + m2
            e1 = jnp.exp(s1 - base)
            e2 = jnp.exp(s2 - base)
            l = jnp.sum(e1, axis=1, keepdims=True) + jnp.sum(e2, axis=1, keepdims=True)
            o_f[which, :, hl] = mm(e1.astype(BF), pv[:, hg]) + mm(e2.astype(BF), tv[:, hg])
            ml = ml_f[which]
            ml = jnp.where(lane_r == hh, base, ml)
            ml_f[which] = jnp.where(lane_r == 3 + hh, l, ml)
            return carry

        lax.fori_loop(low, high, head, 0)

    def pack(ml, lanes):
        first = round_bf(ml)
        second = ml - first
        n = ml.shape[0]
        out = jnp.where(lanes < 6, first, 0.0)
        return jnp.where((lanes >= 64) & (lanes < 70), pltpu.roll(second, 64, 1), out)

    def unpack(t):
        return t + pltpu.roll(t, 64, 1)

    attend(c, 1, 0, 1)
    gathered(9, qac, NC)
    attend(oc, 0, 0, 3)
    oc_s[0, :, :HALF] = o_f[0].astype(BF)
    oc_s[0, :, HALF:] = pack(ml_f[0], lane_r).astype(BF)
    scatter(13, oc_s, oc_r, dev_c, zero, 2)

    attend(c, 1, 1, 3)

    def merge(parts, lanes):
        greatest = parts[0][1]
        for _, ml in parts[1:]:
            greatest = jnp.maximum(greatest, ml)
        sums, totals = [None] * 3, None
        for o, ml in parts:
            f = jnp.exp(ml - greatest)
            t = pltpu.roll(f, 3, 1) * ml
            totals = t if totals is None else totals + t
            for h in range(3):
                term = o[:, h * HD : (h + 1) * HD] * f[:, h : h + 1]
                sums[h] = term if sums[h] is None else sums[h] + term
        return sums, jnp.where(lanes < 3, greatest, totals)

    scattered(13, oc_r)
    sums, ml = merge(
        [
            (o_f[1], jnp.where(lane_r < 6, ml_f[1], 0.0)),
            (
                oc_r[0, :, :HALF].astype(F32),
                jnp.where(lane_r < 6, unpack(oc_r[0, :, HALF:].astype(F32)), 0.0),
            ),
        ],
        lane_r,
    )
    packed = pack(ml, lane_r)
    for h in range(3):
        o_f[0, :, h * HD : (h + 1) * HD] = sums[h]
        op_s[:, :, h * HD : (h + 1) * HD] = sums[h].reshape(PLANE, 8, HD).astype(BF)
    ml_f[0] = ml
    op_s[:, :, HALF:] = packed.reshape(PLANE, 8, 128).astype(BF)
    scatter_p(14, op_s, op_r, same_chip)

    scattered(11, kp_r)
    key = kv_f[0, my_rows, :] + jnp.sum(kp_r[:, 0].astype(F32), axis=0)
    value = kv_f[1, my_rows, :] + jnp.sum(kp_r[:, 1].astype(F32), axis=0)
    key = round_bf(key + qkv_bias[1:2, pl.ds(mine_at, HALF)].astype(F32))
    value = round_bf(value + qkv_bias[2:3, pl.ds(mine_at, HALF)].astype(F32))
    lane_8 = iota((8, 128), 1)
    odd = iota((8, 128), 0) % 2 == 1
    key_before = pltpu.roll(key, 1, 0)
    value_before = pltpu.roll(value, 1, 0)
    same = jnp.full((8, 128), NEG, F32)
    before = jnp.full((8, 128), NEG, F32)
    for h in range(3):
        hs = slice(h * HD, (h + 1) * HD)
        a = jnp.sum(query[:, hs] * key[:, hs], axis=1, keepdims=True) * SCALE
        b = jnp.sum(query[:, hs] * key_before[:, hs], axis=1, keepdims=True) * SCALE
        same = jnp.where(lane_8 == h, a, same)
        before = jnp.where((lane_8 == h) & odd, b, before)

    mine = jnp.where(lane_8 < 6, ml_f[0, my_rows, :], 0.0)
    scattered(14, op_r)
    n31 = (PLANE - 1) * 8
    mls = unpack(op_r[:, :, HALF:].astype(F32).reshape(n31, 128))
    mls = jnp.where(iota((n31, 128), 1) < 6, mls, 0.0)
    ml3 = mls.reshape(PLANE - 1, 8, 128)
    greatest = jnp.maximum(jnp.maximum(jnp.max(ml3, axis=0), mine), jnp.maximum(same, before))
    f3 = jnp.exp(ml3 - greatest[None])
    f = jnp.exp(mine - greatest)
    t3 = (pltpu.roll(f3.reshape(n31, 128), 3, 1) * mls).reshape(PLANE - 1, 8, 128)
    ml = jnp.sum(t3, axis=0) + pltpu.roll(f, 3, 1) * mine
    sums = []
    for h in range(3):
        hs = slice(h * HD, (h + 1) * HD)
        o = jnp.sum(op_r[:, :, hs].astype(F32) * f3[:, :, h : h + 1], axis=0)
        sums.append(o + o_f[0, my_rows, hs] * f[:, h : h + 1])
    w_same = jnp.exp(same - greatest)
    w_before = jnp.exp(before - greatest)
    totals = pltpu.roll(ml, 125, 1) + w_same + w_before
    w_same = round_bf(w_same)
    w_before = round_bf(w_before)
    for h in range(3):
        hs = slice(h * HD, (h + 1) * HD)
        o = sums[h] + w_same[:, h : h + 1] * value[:, hs] + w_before[:, h : h + 1] * value_before[:, hs]
        aap[p, :, hs] = (o / totals[:, h : h + 1]).astype(BF)
    gather_p(16, aap)
    loads[16].wait()
    gathered(16, aap, PLANE)
    aac[c] = aap[...]
    gather(17, aac, c, dev_c, NC)
    gathered(17, aac, NC)
    out = jnp.zeros((R, DL), F32)
    for half in range(2):
        part = aac[half].astype(F32).reshape(R, HALF).astype(BF)
        out = out + mm(part, wo[:, half * HALF : (half + 1) * HALF], NT)
    out = jnp.concatenate([out, jnp.zeros((R, 128 - DL), F32)], axis=1)
    hz_s[...] = out.reshape(NZ, 32, 128).astype(BF)
    scatter(18, hz_s, hz_r, dev_z, to_z, NZ)
    scattered(18, hz_r)
    hidden = hz_s[mz].astype(F32)
    for i in range(7):
        hidden = hidden + hz_r[i].astype(F32)
    hidden = hidden + zi[pair].astype(F32) + gp[4:5, :]
    hs_c[c, 0:1] = to_row(jnp.sum(hidden, axis=1, keepdims=True))
    hs_c[c, 1:2] = to_row(jnp.sum(hidden * hidden, axis=1, keepdims=True))
    gather(19, hs_c, c, dev_c, NC)
    hid[mz] = hidden.astype(BF)
    gathered(19, hs_c, NC)
    hs_p[p] = hs_c[0] + hs_c[1]
    gather_p(20, hs_p)
    gathered(20, hs_p, PLANE)
    total = jnp.sum(hs_p[...], axis=0)
    mean = total[0:1] * (1.0 / D)
    square = total[1:2] * (1.0 / D)
    rstd = lax.rsqrt(square - mean * mean + EPS)
    final = (hidden - to_col(mean, 32)) * to_col(rstd, 32)
    final = (final * gp[1:2, :] + gp[3:4, :]).astype(BF)
    i16 = iota((16, 32), 0)
    last = (iota((16, 32), 1) == 8 * (i16 // 3) + 2 * (i16 % 3) + 1) & (i16 < 12)
    fin[pair] = mm(jnp.where(last, 1.0, 0.0).astype(BF), final).astype(BF)
    gather(22, fin, pair, dev_pair, NP)
    gather(21, hid, mz, dev_z, NZ)
    nrm[mz] = jnp.sqrt(square)
    gather(23, nrm, mz, dev_z, NZ)
    scattered(24, emb_o)
    gathered(22, fin, NP)

    finals = jnp.concatenate([fin[NC * i + c] for i in range(NZ)], axis=0)
    finals_o = jnp.concatenate([fin[NC * i + oc] for i in range(NZ)], axis=0)

    def rows_of(n, start, v):
        cont = iota((n, 128), 0) + start
        hot = iota((n, 128), 1) == (cont // 12) * 16 + cont % 12
        return mm(jnp.where(hot & (cont < CONT), 1.0, 0.0).astype(BF), v).astype(BF)

    full = mm(rows_of(HC, c * HC, finals)[:, :DL], emb[...])
    full = full + mm(rows_of(HC, c * HC, finals_o)[:, :DL], emb_o[...])
    l_f[...] = full
    for t in range(TILES):
        lp_s[t] = full[:, t * 128 : (t + 1) * 128].astype(BF)

    def send_words(j, tx, ty):
        t = tx * NY + ty

        @pl.when(t < TILES)
        def _():
            pltpu.make_async_remote_copy(
                src_ref=lp_s.at[t],
                dst_ref=lp_r.at[j],
                send_sem=ssem.at[25],
                recv_sem=rsem.at[25],
                device_id=dev_chip(tx, ty),
                device_id_type=MESH,
            ).start()

    chips(send_words)
    score = mm(jnp.broadcast_to(gp[5:6, :], (8, 128)).astype(BF), rows_of(128, 0, finals), NT)
    mx_p[p, 1:2] = score[0:1]
    gathered(21, hid, NZ)
    out_row = iota((192, R), 0)
    back = iota((192, R), 1) == (out_row // 6) * 8 + out_row % 6
    states = mm(jnp.where(back, 1.0, 0.0).astype(BF), hid[...].reshape(R, 128))
    hid_out[...] = states[:, :DL].astype(BF)
    gathered(23, nrm, NZ)
    col = iota((128, 192), 1)
    norms = jnp.zeros((1, 192), F32)
    for i in range(NZ):
        at = (col // 6) * 8 + col % 6 - i * 32
        norms = norms + jnp.sum(
            jnp.where(iota((128, 192), 0) == at, to_col(nrm[i], 128), 0.0), axis=0, keepdims=True
        )
    norm_out[...] = norms

    @pl.when(p < TILES)
    def _():
        scattered(25, lp_r)
        logits = l_f[:, pl.ds(pl.multiple_of(p * 128, 128), 128)]
        for i in range(PLANE - 1):
            logits = logits + lp_r[i].astype(F32)
        top = jnp.max(logits, axis=1, keepdims=True)
        lane_h = iota((HC, 128), 1) - c * HC
        top = jnp.sum(jnp.where(lane_h == iota((HC, 128), 0), top, 0.0), axis=0, keepdims=True)
        lane_1 = iota((1, 128), 1) - c * HC
        mx_p[p, 0:1] = jnp.where((lane_1 >= 0) & (lane_1 < HC), top, LOW)

    @pl.when(p >= TILES)
    def _():
        mx_p[p, 0:1] = jnp.full((1, 128), LOW, F32)

    gather_p(30, mx_p)
    gathered(30, mx_p, PLANE)
    mx_z[pair, 0:1] = jnp.max(mx_p[:, 0:1], axis=0)
    mx_z[pair, 1:2] = jnp.sum(mx_p[:, 1:2], axis=0)
    gather(31, mx_z, pair, dev_pair, NP)
    gathered(31, mx_z, NP)
    best = jnp.max(mx_z[:, 0:1], axis=0)
    score_out[...] = (mx_z[0, 1:2] + mx_z[1, 1:2])[:, :CONT]
    top_out[...] = best[:, :CONT]

    @pl.when(p < TILES)
    def _():
        part = lp_s.at[pl.ds(0, TILES - 1)]
        pltpu.make_async_copy(part, part, ssem.at[25]).wait()

    @pl.when(p >= TILES)
    def _():
        pltpu.make_async_copy(lp_s, lp_s, ssem.at[25]).wait()

    for s, part in waits:
        pltpu.make_async_copy(part, part, ssem.at[s]).wait()


def per_device(
    token_ids,
    prompt_lengths,
    tail_lengths,
    prompt_of,
    page_table,
    prompt_keys,
    prompt_values,
    tail_keys,
    tail_values,
    norm_gain,
    norm_bias,
    qkv_weight,
    qkv_bias,
    out_weight,
    out_bias,
    embedding,
    score_weight,
):
    vm = pl.BlockSpec(memory_space=pltpu.VMEM)
    hbm = pl.BlockSpec(memory_space=pl.ANY)

    def b(*shape):
        return pltpu.VMEM(shape, BF)

    def f(*shape):
        return pltpu.VMEM(shape, F32)

    i32 = jnp.int32
    scratch = [
        pltpu.VMEM((1, 6), i32),
        pltpu.VMEM((2, CONT), i32),
        pltpu.VMEM((1, CONT), i32),
        pltpu.VMEM((1, CONT), i32),
        pltpu.VMEM((2, CONT), i32),
        b(2, DL),
        b(2, DL),
        b(3, 768),
        b(1, DL),
        b(1, DL),
        b(768, 768),
        b(768, 768),
        b(384, 768),
        b(384, 768),
        b(3, DL, 768),
        b(DL, 768),
        b(DL, VL),
        f(R, 1152),
        b(NC, R, 128),
        f(8, 128),
        b(8, 32, 128),
        b(7, 32, 128),
        b(NP, 32, 128),
        f(8, 128),
        b(3, DL, HALF),
        b(DL, VL),
        f(PLANE, 4, 128),
        f(NP, 4, 128),
        f(R, HALF),
        b(PLANE, 8, HALF),
        b(PLANE - 1, 8, HALF),
        b(PLANE, 8, HALF),
        b(NC, PLANE, 8, HALF),
        f(2, R, HALF),
        b(PLANE, 2, 8, HALF),
        b(PLANE - 1, 2, 8, HALF),
        f(2, R, HALF),
        f(2, R, 128),
        b(1, R, 512),
        b(1, R, 512),
        b(PLANE, 8, 512),
        b(PLANE - 1, 8, 512),
        b(PLANE, 8, HALF),
        b(NC, PLANE, 8, HALF),
        b(8, 32, 128),
        b(7, 32, 128),
        f(NC, 2, 128),
        f(PLANE, 2, 128),
        b(8, 32, 128),
        b(NP, 16, 128),
        f(NZ, 1, 128),
        f(HC, VL),
        b(TILES, HC, 128),
        b(PLANE - 1, HC, 128),
        f(PLANE, 2, 128),
        f(NP, 2, 128),
        pltpu.SemaphoreType.DMA((32,)),
        pltpu.SemaphoreType.DMA((32,)),
        pltpu.SemaphoreType.DMA((17,)),
    ]
    hidden, score, norms, top = pl.pallas_call(
        kernel,
        out_shape=(
            jax.ShapeDtypeStruct((192, DL), BF),
            jax.ShapeDtypeStruct((1, CONT), F32),
            jax.ShapeDtypeStruct((1, 192), F32),
            jax.ShapeDtypeStruct((1, CONT), F32),
        ),
        in_specs=[hbm] * 17,
        out_specs=(vm, vm, vm, vm),
        scratch_shapes=scratch,
        compiler_params=pltpu.CompilerParams(
            collective_id=0, has_side_effects=True, vmem_limit_bytes=60 * 2**20
        ),
    )(
        prompt_lengths.reshape(1, 6),
        token_ids.T,
        tail_lengths.reshape(1, CONT),
        prompt_of.reshape(1, CONT),
        page_table.T,
        norm_gain,
        norm_bias,
        qkv_bias,
        out_bias.reshape(1, DL),
        score_weight.reshape(1, DL),
        prompt_keys,
        prompt_values,
        tail_keys,
        tail_values,
        qkv_weight.transpose(1, 0, 2),
        out_weight.T,
        embedding.T,
    )
    return hidden, score.reshape(CONT), norms.reshape(192), top.reshape(CONT)


def solution(mesh):
    return jax.shard_map(
        per_device,
        mesh=mesh,
        in_specs=(
            P(),
            P(),
            P(),
            P(),
            P(),
            P("seq", "mp"),
            P("seq", "mp"),
            P("seq", "mp"),
            P("seq", "mp"),
            P(None, "seq"),
            P(None, "seq"),
            P("seq", None, "mp"),
            P(None, "mp"),
            P("mp", "seq"),
            P("seq"),
            P("mp", "seq"),
            P("seq"),
        ),
        out_specs=(P(None, "seq"), P(), P(), P()),
        check_vma=False,
    )
```

time: 147 us -> 113 us (0.77)
  Pallas kernels: 129 us -> 107 us
  local copies, waits for them, and re-layouts: 16.6 us -> 4.84 us
    pallas_call x1, Pallas kernels: 129 us -> 107 us  [per_device(): pl.pallas_call(kernel, out_shape=(jax.ShapeDtypeStruct((192, DL), BF), ja...]
    unnamed x38 -> x4, local copies, waits for them, and re-layouts: 16.6 us -> 4.84 us
where the time goes in v2:
time: 113 us
  Pallas kernels  107 us (95%)
  local copies, waits for them, and re-layouts  4.84 us (4%)
    pallas_call x1, Pallas kernels, per_device(): pl.pallas_call(kernel, out_shape=(jax.ShapeDtypeStruct((192, DL), BF), ja...  107 us
    unnamed x4, local copies, waits for them, and re-layouts  4.84 us

profile of v2, /device:TPU:1, one launch (start us, length us, event | category | flops | bytes accessed | tf_op | source)
XLA Modules:
  0.0 112.8 jit_solution(6935174562839471762)
XLA Ops:
  0.6 107.3 %shard_map.192 = (bf16[192,112]{1,0:T(8,128)(2,1)}, f32[1,96]{1,0:T(1,128)}, f32[1,192]{1,0:T(1,128)}, f32[1,96]{1,0:T(1,128)}) custom-call(s32[1,6]{1,0:T(1,128)} %bitcast.19, s32[2,96]{1,0:T(2,128)} %bitcast.16, s32[1,96]{1,0:T(1,128)} %bitcast.20, s32[1,96]{1,0:T(1,128)} %bitcast.21, s32[2,96]{1,0:T(2,128)} %bitcast.17, bf16[2,112]{1,0:T(2,128)(2,1)} %gain_hbm.1, ...), custom_call_target="tpu_custom_call" | custom-call | tf_op jit(solution)/shard_map/pallas_call | solution.py:749
  107.9 1.4 %copy.25 = bf16[192,112]{1,0:T(8,128)(2,1)} copy(bf16[192,112]{1,0:T(8,128)(2,1)} %get-tuple-element.16) | data formatting | bytes 86016
  109.4 1.1 copy.26
  110.5 1.2 %copy.27 = f32[192]{0:T(256)} copy(f32[192]{0:T(256)} %bitcast.18) | data formatting | bytes 1536
  111.7 1.1 copy.28
